TPU v7x, 32 devices: a whole 2x2x4 slice. The times are simulated.
32 devices in a mesh: span: 4 (over z), shard: 8 (over y, x, core).
Axes of the slice: x: 2, y: 2, z: 4, core: 2. Of those that a mesh axis runs over, the one named last changes fastest.
Arguments:
- tokens: bfloat16 [8192, 1152], P(('span', 'shard')), may hold values from -6 to 6
- out_proj: bfloat16 [1152, 1152], replicated, may hold values from -0.1875 to 0.1875
- phi_mean: float32 [1152], replicated, may hold values from -6 to 6
- phi_rotate: bfloat16 [1152, 576], replicated, may hold values from -0.1875 to 0.1875
- destinations: int32 [8192, 1], P(('span', 'shard')), may hold values from 0 to 3; in each aligned block of 256 rows (0 to 255, 256 to 511, ...) at most 96 rows name the same one
- student_hidden: bfloat16 [12288, 1280], P(('span', 'shard')), may hold values from -6 to 6
- adaptor: bfloat16 [1280, 576], replicated, may hold values from -0.15625 to 0.15625
- master: float32 [1280, 576], P('shard'), may hold values from -0.15625 to 0.15625
- moment_one: float32 [1280, 576], P('shard'), may hold values from -4 to 4
- moment_two: float32 [1280, 576], P('shard'), may hold values from 0.01 to 1
Outputs:
- updated_master: float32 [1280, 576], P('shard')
- updated_first: float32 [1280, 576], P('shard')
- updated_second: float32 [1280, 576], P('shard')
Inputs may be any that keep to these rules, and one draw needn't show every extreme that they name: `destinations`: at most 96 of the 256 rows of one device name one span; some span gets exactly 96.
All inputs are finite; a program needn't handle non-finite values.
Results may differ from a plain program's by a relative error of at most 0.00064.
Values may be sent and summed in bfloat16 or wider, within the bound.
A program may use at most 64 MiB of HBM per device.

v0:
```python
import functools

import jax
import jax.numpy as jnp
from jax import lax
from jax.experimental import pallas as pl
from jax.experimental.pallas import tpu as pltpu
from jax.sharding import PartitionSpec as P

ADAM_STEP = 1000


beta_first = 0.9
beta_second = 0.999
adam_epsilon = 1e-08
decay_rate = 0.05
learn_rate = 0.001

EMPTY = 2.0**100
EMPTY_TEST = 2.0**90
MESH = pl.DeviceIdType.MESH


def adam_update(gradient, master, moment_one, moment_two):
    first_new = beta_first * moment_one + (1.0 - beta_first) * gradient
    second_new = beta_second * moment_two + (1.0 - beta_second) * gradient * gradient
    bias_first = 1.0 - beta_first**ADAM_STEP
    bias_second = 1.0 - beta_second**ADAM_STEP
    update_dir = (
        first_new / bias_first / (jnp.sqrt(second_new / bias_second) + adam_epsilon)
        + decay_rate * master
    )
    return (master - learn_rate * update_dir, first_new, second_new)


def route_slots(destinations, span_count, capacity):
    target_span = destinations[:, 0]
    span_ids = jnp.arange(span_count, dtype=jnp.int32)
    one_hot = (target_span[:, None] == span_ids[None, :]).astype(jnp.int32)
    before = jnp.cumsum(one_hot, axis=0) - one_hot
    slot_rank = jnp.sum(before * one_hot, axis=1)
    return target_span * capacity + slot_rank


def general_body(
    tokens,
    out_proj,
    phi_mean,
    phi_rotate,
    destinations,
    student_hidden,
    adaptor,
    master,
    moment_one,
    moment_two,
):
    span_count = lax.axis_size("span")
    slots = student_hidden.shape[0]
    capacity = slots // span_count
    features = adaptor.shape[1]
    projected = (jnp.dot(tokens, out_proj, preferred_element_type=jnp.float32) - phi_mean).astype(
        jnp.bfloat16
    )
    target = jnp.dot(projected, phi_rotate, preferred_element_type=jnp.float32).astype(jnp.bfloat16)
    slot_ids = route_slots(destinations, span_count, capacity)
    placed = jnp.full((slots, features), EMPTY, jnp.bfloat16).at[slot_ids].set(target)
    arrived = lax.all_to_all(
        placed.reshape(span_count, capacity, features), "span", split_axis=0, concat_axis=0, tiled=True
    ).reshape(slots, features)
    activated = jax.nn.gelu(student_hidden.astype(jnp.float32), approximate=False).astype(jnp.bfloat16)
    predicted = jnp.dot(activated, adaptor, preferred_element_type=jnp.float32)
    wanted = arrived.astype(jnp.float32)
    scaled_error = jnp.where(wanted > EMPTY_TEST, 0.0, (predicted - wanted) / features).astype(
        jnp.bfloat16
    )
    contract = (((0,), (0,)), ((), ()))
    partial_sum = lax.psum_scatter(
        lax.dot_general(activated, scaled_error, contract, preferred_element_type=jnp.float32),
        "shard",
        scatter_dimension=0,
        tiled=True,
    )
    return adam_update(lax.psum(partial_sum, "span"), master, moment_one, moment_two)


SPANS = 4
SHARDS = 8


def chunks_of(features):
    return tuple((lo, min(lo + 128, features)) for lo in range(0, features, 128))


def dot(a, b):
    return jnp.dot(a, b, preferred_element_type=jnp.float32)


def dot_t(a, b):
    return lax.dot_general(a, b, (((1,), (1,)), ((), ())), preferred_element_type=jnp.float32)


def encode(values, codes, scale):
    top = jnp.max(jnp.max(jnp.abs(values), axis=0, keepdims=True), axis=1, keepdims=True)
    top = jnp.maximum(top, 1e-30)
    codes[...] = jnp.round(values * (32000.0 / top)).astype(jnp.int32).astype(jnp.int16)
    scale[...] = jnp.broadcast_to(top * (1.0 / 32000.0), scale.shape)


def decode(codes, scale):
    return codes[...].astype(jnp.int32).astype(jnp.float32) * scale[0:1, 0:1]


def step_kernel(
    chunks,
    tokens_hbm,
    proj_hbm,
    mean_hbm,
    rotate_hbm,
    dest_hbm,
    hidden_hbm,
    adaptor_hbm,
    out,
    tokens,
    proj,
    mean,
    rotate,
    dest,
    hidden,
    adaptor,
    act,
    act_t,
    pred,
    *rest,
):
    per_chunk, (load_sem, a2a_send, a2a_recv, core_sem, plane_send, plane_recv, z_sem) = (
        rest[:-7],
        rest[-7:],
    )
    count = len(per_chunk) // len(chunks)
    buf = [per_chunk[c * count : (c + 1) * count] for c in range(len(chunks))]

    span = lax.axis_index("span")
    me = lax.axis_index("shard")
    core = lax.rem(me, 2)
    my_x = lax.rem(me // 2, 2)
    my_y = me // 4
    core_mate = me + 1 - 2 * core
    x_mate = me + 2 - 4 * my_x
    y_mate = me + 4 - 8 * my_y
    cross_mate = y_mate + 2 - 4 * my_x
    plane_mates = (x_mate, y_mate, cross_mate)
    z_mates = (span + 1 - 2 * lax.rem(span, 2), span + 2 - 4 * (span // 2))
    z_low = (lax.rem(span, 2) == 0, span < 2)

    slots, width = hidden.shape
    rows = tokens.shape[0]
    features = adaptor.shape[0]
    cap = slots // SPANS
    block = width // SHARDS

    pairs = (
        (tokens_hbm, tokens),
        (proj_hbm, proj),
        (mean_hbm, mean),
        (dest_hbm, dest),
        (rotate_hbm, rotate),
        (hidden_hbm, hidden),
        (adaptor_hbm, adaptor),
    )
    loads = [pltpu.make_async_copy(s, d, load_sem.at[i]) for i, (s, d) in enumerate(pairs)]
    for i in (0, 1, 2, 3, 4):
        loads[i].start()

    barrier = pltpu.get_barrier_semaphore()
    for step in range(1, SPANS):
        pl.semaphore_signal(
            barrier, inc=1, device_id=(lax.rem(span + step, SPANS), me), device_id_type=MESH
        )
    for mate in (core_mate, *plane_mates):
        pl.semaphore_signal(barrier, inc=1, device_id=(span, mate), device_id_type=MESH)

    loads[3].wait()
    wanted = dest[...]
    span_ids = lax.broadcasted_iota(jnp.int32, (16, rows), 0)
    one_hot = jnp.where(span_ids == wanted, 1.0, 0.0)
    earlier = jnp.where(
        lax.broadcasted_iota(jnp.int32, (rows, rows), 0)
        < lax.broadcasted_iota(jnp.int32, (rows, rows), 1),
        1.0,
        0.0,
    ).astype(jnp.bfloat16)
    before = dot(one_hot.astype(jnp.bfloat16), earlier)
    rank = jnp.sum(before * one_hot, axis=0, keepdims=True).astype(jnp.int32)
    slot = wanted * cap + rank
    place = jnp.where(lax.broadcasted_iota(jnp.int32, (slots, rows), 0) == slot, 1.0, 0.0)
    empty = (1.0 - jnp.sum(place, axis=1, keepdims=True)) * EMPTY
    place = place.astype(jnp.bfloat16)

    for i in (0, 1, 2):
        loads[i].wait()
    projected = (dot(tokens[...], proj[...]) - mean[...].reshape(1, -1)).astype(jnp.bfloat16)
    for i in (5, 6):
        loads[i].start()
    loads[4].wait()
    pl.semaphore_wait(barrier, SPANS - 1 + 4)

    a2a = []
    for c, (lo, hi) in enumerate(chunks):
        t_send, t_recv = buf[c][0], buf[c][1]
        target = dot_t(projected, rotate[lo:hi, :]).astype(jnp.bfloat16)
        t_send[...] = (dot(place, target) + empty).astype(jnp.bfloat16)
        for step in (2, 3, 1):
            other = lax.rem(span + step, SPANS)
            copy = pltpu.make_async_remote_copy(
                src_ref=t_send.at[pl.ds(pl.multiple_of(other * cap, 16), cap)],
                dst_ref=t_recv.at[pl.ds(pl.multiple_of(span * cap, 16), cap)],
                send_sem=a2a_send.at[c, step - 1],
                recv_sem=a2a_recv.at[c, step - 1],
                device_id=(other, me),
                device_id_type=MESH,
            )
            copy.start()
            a2a.append(copy)
        mine = pl.ds(pl.multiple_of(span * cap, 16), cap)
        t_recv[mine, :] = t_send[mine, :]

    loads[5].wait()
    for j in range(0, width, 128):
        x = hidden[:, j : j + 128].astype(jnp.float32)
        a = (0.5 * x * (1.0 + lax.erf(x * (0.5**0.5)))).astype(jnp.bfloat16)
        act[:, j : j + 128] = a
        act_t[j : j + 128, :] = a.T
    loads[6].wait()
    pred[...] = dot_t(act[...], adaptor[...])

    sends = []

    def send(src, dst, send_sem, recv_sem, device):
        copy = pltpu.make_async_remote_copy(
            src_ref=src,
            dst_ref=dst,
            send_sem=send_sem,
            recv_sem=recv_sem,
            device_id=device,
            device_id_type=MESH,
        )
        copy.start()
        return copy

    class Pair:
        def __init__(self, c, src, dst, sems, device):
            self.copies = [
                pltpu.make_async_remote_copy(
                    src_ref=buf[c][src + 4 * i],
                    dst_ref=buf[c][dst + 4 * i],
                    send_sem=sems[i],
                    recv_sem=sems[2 + i],
                    device_id=device,
                    device_id_type=MESH,
                )
                for i in range(2)
            ]

        def start(self):
            for copy in self.copies:
                copy.start()

        def wait_recv(self):
            for copy in self.copies:
                copy.wait_recv()

        def wait_send(self):
            for copy in self.copies:
                copy.wait_send()

    def put(values, c, at):
        encode(values, buf[c][at], buf[c][at + 4])

    def get(c, at):
        return decode(buf[c][at], buf[c][at + 4])

    core_copies = {}
    plane_copies = {}
    z_copies = {}

    def gradient_block(index, error):
        start = pl.multiple_of(index * block, 16)
        return dot(act_t[pl.ds(start, block), :], error)

    def form(c):
        lo, hi = chunks[c]
        t_recv, core_out, core_in, total = buf[c][1], buf[c][2], buf[c][3], buf[c][4]
        for copy in a2a[3 * c : 3 * c + 3]:
            copy.wait_recv()
        t = t_recv[...].astype(jnp.float32)
        error = jnp.where(t > EMPTY_TEST, 0.0, (pred[:, lo:hi] - t) * (1.0 / features)).astype(
            jnp.bfloat16
        )
        for j in range(4):
            core_out[j] = gradient_block(2 * j + 1 - core, error).astype(jnp.bfloat16)
        core_copies[c] = send(
            core_out, core_in, core_sem.at[c, 0], core_sem.at[c, 1], (span, core_mate)
        )
        for j in range(4):
            total[j] = gradient_block(2 * j + core, error)

    def plane(c):
        core_in, total, plane_out, plane_in = buf[c][3], buf[c][4], buf[c][5], buf[c][6]
        core_copies[c].wait_recv()
        for j, mate in enumerate(plane_mates):
            away = mate // 2
            plane_out[j] = (total[away] + core_in[away]).astype(jnp.bfloat16)
            plane_copies[c, j] = send(
                plane_out.at[j],
                plane_in.at[j],
                plane_send.at[c, j],
                plane_recv.at[c, j],
                (span, mate),
            )

    def z_send(c, stage):
        at = 7 + 2 * stage
        z_copies[c, stage] = Pair(
            c, at, at + 1, [z_sem.at[c, stage, i] for i in range(4)], (z_mates[stage], me)
        )
        z_copies[c, stage].start()

    def z_sum(c, stage):
        at = 7 + 2 * stage
        z_copies[c, stage].wait_recv()
        mine, other = get(c, at), get(c, at + 1)
        low = jnp.where(z_low[stage], mine, other)
        high = jnp.where(z_low[stage], other, mine)
        return low + high

    def first_z(c):
        core_in, total, plane_in = buf[c][3], buf[c][4], buf[c][6]
        here = me // 2
        own = total[here] + core_in[here]
        for j in range(3):
            plane_copies[c, j].wait_recv()
            own = own + plane_in[j]
        put(own, c, 7)
        z_send(c, 0)

    def second_z(c):
        put(z_sum(c, 0), c, 9)
        z_send(c, 1)

    def finish(c):
        lo, hi = chunks[c]
        out[:, lo:hi] = z_sum(c, 1)

    n = len(chunks)
    for c in range(n):
        form(c)
        if c >= 1:
            first_z(c - 1)
        if c >= 2:
            second_z(c - 2)
        plane(c)
        if c >= 3:
            finish(c - 3)
    second_z(n - 2)
    first_z(n - 1)
    finish(n - 3)
    finish(n - 2)
    second_z(n - 1)
    finish(n - 1)

    for copy in a2a:
        copy.wait_send()
    for group in (core_copies, plane_copies, z_copies):
        for copy in group.values():
            copy.wait_send()


def kernel_body(
    tokens,
    out_proj,
    phi_mean,
    phi_rotate,
    destinations,
    student_hidden,
    adaptor,
    master,
    moment_one,
    moment_two,
):
    rows = tokens.shape[0]
    slots, width = student_hidden.shape
    features = adaptor.shape[1]
    block = width // SHARDS
    chunks = chunks_of(features)
    bf16, f32 = jnp.bfloat16, jnp.float32
    dest = destinations.reshape(1, rows)
    inputs = (
        tokens,
        out_proj,
        phi_mean,
        phi_rotate.T,
        dest,
        student_hidden,
        adaptor.T,
    )
    scratch = [pltpu.VMEM(a.shape, a.dtype) for a in inputs]
    scratch += [
        pltpu.VMEM((slots, width), bf16),
        pltpu.VMEM((width, slots), bf16),
        pltpu.VMEM((slots, features), f32),
    ]
    for lo, hi in chunks:
        wide = hi - lo
        scratch += [pltpu.VMEM((slots, wide), bf16)] * 2
        scratch += [pltpu.VMEM((4, block, wide), bf16)] * 2
        scratch += [pltpu.VMEM((4, block, wide), f32)]
        scratch += [pltpu.VMEM((3, block, wide), bf16)] * 2
        scratch += [pltpu.VMEM((block, wide), jnp.int16)] * 4
        scratch += [pltpu.VMEM((8, 128), f32)] * 4
    n = len(chunks)
    dma = pltpu.SemaphoreType.DMA
    scratch += [
        dma((len(inputs),)),
        dma((n, SPANS - 1)),
        dma((n, SPANS - 1)),
        dma((n, 2)),
        dma((n, 3)),
        dma((n, 3)),
        dma((n, 2, 4)),
    ]
    flops = 2 * (rows * tokens.shape[1] * (tokens.shape[1] + features) + 2 * slots * width * features)
    gradient = pl.pallas_call(
        functools.partial(step_kernel, chunks),
        out_shape=jax.ShapeDtypeStruct(master.shape, f32),
        in_specs=[pl.BlockSpec(memory_space=pl.ANY)] * len(inputs),
        out_specs=pl.BlockSpec(memory_space=pltpu.VMEM),
        scratch_shapes=scratch,
        compiler_params=pltpu.CompilerParams(
            collective_id=0, has_side_effects=True, vmem_limit_bytes=62 * 2**20
        ),
        cost_estimate=pl.CostEstimate(
            flops=flops, bytes_accessed=10 * 2**20, transcendentals=slots * width
        ),
    )(*inputs)
    return adam_update(gradient, master, moment_one, moment_two)


def solution(mesh):
    in_specs = (
        P(("span", "shard"), None),
        P(),
        P(),
        P(),
        P(("span", "shard"), None),
        P(("span", "shard"), None),
        P(),
        P("shard", None),
        P("shard", None),
        P("shard", None),
    )
    out_specs = (P("shard", None), P("shard", None), P("shard", None))
    tuned = mesh.shape["span"] == SPANS and mesh.shape["shard"] == SHARDS
    body = kernel_body if tuned else general_body
    return jax.shard_map(body, mesh=mesh, in_specs=in_specs, out_specs=out_specs, check_vma=False)
```

profile of v0, /device:TPU:0, one launch (start us, length us, event | category | flops | bytes accessed | tf_op | source)
XLA Modules:
  0.0 47.1 jit_solution(11334414724122055717)
XLA Ops:
  0.6 0.0 copy-start
  0.6 0.0 copy-start.1
  0.7 0.0 copy-start.2
  0.7 44.2 %shard_map.121 = f32[160,576]{1,0:T(8,128)} custom-call(bf16[256,1152]{1,0:T(8,128)(2,1)} %tokens_hbm.1, bf16[1152,1152]{1,0:T(8,128)(2,1)} %proj_hbm.1, f32[1152]{0:T(1024)} %mean_hbm.1, bf16[576,1152]{1,0:T(8,128)(2,1)} %bitcast.4, s32[1,256]{1,0:T(1,128)} %bitcast.5, bf16[384,1280]{1,0:T(8,128)(2,1)} %hidden_hbm.1, bf16[576,1280]{1,0:T(8,128)(2,1)} %bitcast.3), custom_call_target="tpu_custom_call" | custom-call | flops 2151677952 | bytes 10485760 | tf_op jit(solution)/shard_map/pallas_call | solution.py:432
  44.9 0.0 copy-done
  44.9 0.0 copy-done.1
  44.9 0.0 copy-done.2
  44.9 2.2 %multiply_subtract_fusion = (f32[160,576]{1,0:T(8,128)}, f32[160,576]{1,0:T(8,128)}, f32[160,576]{1,0:T(8,128)}) fusion(f32[160,576]{1,0:T(8,128)S(1)} %copy-done, f32[160,576]{1,0:T(8,128)} %shard_map.121, f32[160,576]{1,0:T(8,128)S(1)} %copy-done.1, f32[160,576]{1,0:T(8,128)S(1)} %copy-done.2), kind=kLoop, calls=%fused_computation.2 | loop fusion | flops 1290240 | bytes 2580480 | tf_op jit(solution)/shard_map/sub | solution.py:33
Async XLA Ops:
  0.6 44.2 %copy-start = (f32[160,576]{1,0:T(8,128)S(1)}, f32[160,576]{1,0:T(8,128)}, u32[]{:S(2)}) copy-start(f32[160,576]{1,0:T(8,128)} %param.17) | copy-start | bytes 1105924
  0.6 44.2 %copy-start.1 = (f32[160,576]{1,0:T(8,128)S(1)}, f32[160,576]{1,0:T(8,128)}, u32[]{:S(2)}) copy-start(f32[160,576]{1,0:T(8,128)} %param.19) | copy-start | bytes 1105924
  0.7 44.2 %copy-start.2 = (f32[160,576]{1,0:T(8,128)S(1)}, f32[160,576]{1,0:T(8,128)}, u32[]{:S(2)}) copy-start(f32[160,576]{1,0:T(8,128)} %param.18) | copy-start | bytes 1105924
where the time goes:
time: 47.3 us; the launch traced here: 47.1 us
  Pallas kernels  44.2 us (93%)
  other arithmetic  2.2 us (5%)
  between operations  0.69 us (1%)
    pallas_call x1, Pallas kernels, kernel_body(): pl.pallas_call(functools.partial(step_kernel, chunks), out_shape=jax.Shap...  44.2 us
    sub x1, other arithmetic, adam_update(): return (master - learn_rate * update_dir, first_new, second_new)  2.2 us

commit v1 on v0

--- a/solution.py
+++ b/solution.py
@@ -150,13 +150,14 @@
     cross_mate = y_mate + 2 - 4 * my_x
     plane_mates = (x_mate, y_mate, cross_mate)
     z_mates = (span + 1 - 2 * lax.rem(span, 2), span + 2 - 4 * (span // 2))
-    z_low = (lax.rem(span, 2) == 0, span < 2)
 
     slots, width = hidden.shape
     rows = tokens.shape[0]
     features = adaptor.shape[0]
     cap = slots // SPANS
     block = width // SHARDS
+    group = width // 2
+    half = block // 2
 
     pairs = (
         (tokens_hbm, tokens),
@@ -229,7 +230,15 @@
         x = hidden[:, j : j + 128].astype(jnp.float32)
         a = (0.5 * x * (1.0 + lax.erf(x * (0.5**0.5)))).astype(jnp.bfloat16)
         act[:, j : j + 128] = a
-        act_t[j : j + 128, :] = a.T
+        a_t = a.T
+        at = j
+        while at < j + 128:
+            index = at // block
+            end = min(j + 128, (index + 1) * block)
+            own_core = core if index % 2 == 1 else 1 - core
+            to = own_core * group + index // 2 * block + at % block
+            act_t[pl.ds(pl.multiple_of(to, 16), end - at), :] = a_t[at - j : end - j, :]
+            at = end
     loads[6].wait()
     pred[...] = dot_t(act[...], adaptor[...])
 
@@ -251,8 +260,8 @@
         def __init__(self, c, src, dst, sems, device):
             self.copies = [
                 pltpu.make_async_remote_copy(
-                    src_ref=buf[c][src + 4 * i],
-                    dst_ref=buf[c][dst + 4 * i],
+                    src_ref=buf[c][src + 6 * i],
+                    dst_ref=buf[c][dst + 6 * i],
                     send_sem=sems[i],
                     recv_sem=sems[2 + i],
                     device_id=device,
@@ -274,18 +283,17 @@
                 copy.wait_send()
 
     def put(values, c, at):
-        encode(values, buf[c][at], buf[c][at + 4])
+        encode(values, buf[c][at], buf[c][at + 6])
 
     def get(c, at):
-        return decode(buf[c][at], buf[c][at + 4])
+        return decode(buf[c][at], buf[c][at + 6])
 
     core_copies = {}
     plane_copies = {}
     z_copies = {}
 
-    def gradient_block(index, error):
-        start = pl.multiple_of(index * block, 16)
-        return dot(act_t[pl.ds(start, block), :], error)
+    def rows_of(index):
+        return pl.ds(pl.multiple_of(index * block, 16), block)
 
     def form(c):
         lo, hi = chunks[c]
@@ -296,20 +304,18 @@
         error = jnp.where(t > EMPTY_TEST, 0.0, (pred[:, lo:hi] - t) * (1.0 / features)).astype(
             jnp.bfloat16
         )
-        for j in range(4):
-            core_out[j] = gradient_block(2 * j + 1 - core, error).astype(jnp.bfloat16)
+        core_out[...] = dot(act_t[:group, :], error).astype(jnp.bfloat16)
         core_copies[c] = send(
             core_out, core_in, core_sem.at[c, 0], core_sem.at[c, 1], (span, core_mate)
         )
-        for j in range(4):
-            total[j] = gradient_block(2 * j + core, error)
+        total[...] = dot(act_t[group:, :], error)
 
     def plane(c):
         core_in, total, plane_out, plane_in = buf[c][3], buf[c][4], buf[c][5], buf[c][6]
         core_copies[c].wait_recv()
         for j, mate in enumerate(plane_mates):
-            away = mate // 2
-            plane_out[j] = (total[away] + core_in[away]).astype(jnp.bfloat16)
+            away = rows_of(mate // 2)
+            plane_out[j] = (total[away, :] + core_in[away, :]).astype(jnp.bfloat16)
             plane_copies[c, j] = send(
                 plane_out.at[j],
                 plane_in.at[j],
@@ -321,35 +327,43 @@
     def z_send(c, stage):
         at = 7 + 2 * stage
         z_copies[c, stage] = Pair(
-            c, at, at + 1, [z_sem.at[c, stage, i] for i in range(4)], (z_mates[stage], me)
+            c, at, at + 1, [z_sem.at[c, stage, i] for i in range(4)], (z_mates[stage % 2], me)
         )
         z_copies[c, stage].start()
 
-    def z_sum(c, stage):
-        at = 7 + 2 * stage
-        z_copies[c, stage].wait_recv()
-        mine, other = get(c, at), get(c, at + 1)
-        low = jnp.where(z_low[stage], mine, other)
-        high = jnp.where(z_low[stage], other, mine)
-        return low + high
+    odd = lax.rem(span, 2)
+    kept_half = pl.ds(pl.multiple_of(odd * half, 16), half)
+    given_half = pl.ds(pl.multiple_of((1 - odd) * half, 16), half)
 
     def first_z(c):
-        core_in, total, plane_in = buf[c][3], buf[c][4], buf[c][6]
-        here = me // 2
-        own = total[here] + core_in[here]
+        core_in, total, plane_in, own = buf[c][3], buf[c][4], buf[c][6], buf[c][19]
+        here = rows_of(me // 2)
+        value = total[here, :] + core_in[here, :]
         for j in range(3):
             plane_copies[c, j].wait_recv()
-            own = own + plane_in[j]
-        put(own, c, 7)
+            value = value + plane_in[j]
+        own[...] = value
+        put(own[given_half, :], c, 7)
         z_send(c, 0)
 
     def second_z(c):
-        put(z_sum(c, 0), c, 9)
+        z_copies[c, 0].wait_recv()
+        put(buf[c][19][kept_half, :] + get(c, 8), c, 9)
         z_send(c, 1)
+
+    def third_z(c):
+        z_copies[c, 1].wait_recv()
+        mine, other = get(c, 9), get(c, 10)
+        low = jnp.where(span < 2, mine, other)
+        high = jnp.where(span < 2, other, mine)
+        put(low + high, c, 11)
+        z_send(c, 2)
 
     def finish(c):
         lo, hi = chunks[c]
-        out[:, lo:hi] = z_sum(c, 1)
+        z_copies[c, 2].wait_recv()
+        out[kept_half, lo:hi] = get(c, 11)
+        out[given_half, lo:hi] = get(c, 12)
 
     n = len(chunks)
     for c in range(n):
@@ -360,13 +374,13 @@
             second_z(c - 2)
         plane(c)
         if c >= 3:
-            finish(c - 3)
-    second_z(n - 2)
-    first_z(n - 1)
-    finish(n - 3)
-    finish(n - 2)
-    second_z(n - 1)
-    finish(n - 1)
+            third_z(c - 3)
+        if c >= 4:
+            finish(c - 4)
+    for c in range(n, n + 4):
+        for stage, step in ((2, second_z), (1, first_z), (3, third_z), (4, finish)):
+            if 0 <= c - stage < n:
+                step(c - stage)
 
     for copy in a2a:
         copy.wait_send()
@@ -412,11 +426,12 @@
     for lo, hi in chunks:
         wide = hi - lo
         scratch += [pltpu.VMEM((slots, wide), bf16)] * 2
-        scratch += [pltpu.VMEM((4, block, wide), bf16)] * 2
-        scratch += [pltpu.VMEM((4, block, wide), f32)]
+        scratch += [pltpu.VMEM((width // 2, wide), bf16)] * 2
+        scratch += [pltpu.VMEM((width // 2, wide), f32)]
         scratch += [pltpu.VMEM((3, block, wide), bf16)] * 2
-        scratch += [pltpu.VMEM((block, wide), jnp.int16)] * 4
-        scratch += [pltpu.VMEM((8, 128), f32)] * 4
+        scratch += [pltpu.VMEM((block // 2, wide), jnp.int16)] * 6
+        scratch += [pltpu.VMEM((8, 128), f32)] * 6
+        scratch += [pltpu.VMEM((block, wide), f32)]
     n = len(chunks)
     dma = pltpu.SemaphoreType.DMA
     scratch += [
@@ -426,7 +441,7 @@
         dma((n, 2)),
         dma((n, 3)),
         dma((n, 3)),
-        dma((n, 2, 4)),
+        dma((n, 3, 4)),
     ]
     flops = 2 * (rows * tokens.shape[1] * (tokens.shape[1] + features) + 2 * slots * width * features)
     gradient = pl.pallas_call(

time: 47.3 us -> 49.4 us (1.044)
  Pallas kernels: 44.2 us -> 46.4 us
    pallas_call x1, Pallas kernels: 44.2 us -> 46.4 us  [kernel_body(): pl.pallas_call(functools.partial(step_kernel, chunks), out_shape=jax.Shap...]
where the time goes in v1:
time: 49.4 us; the launch traced here: 49.3 us
  Pallas kernels  46.4 us (94%)
  other arithmetic  2.2 us (4%)
  between operations  0.69 us (1%)
    pallas_call x1, Pallas kernels, kernel_body(): pl.pallas_call(functools.partial(step_kernel, chunks), out_shape=jax.Shap...  46.4 us
    sub x1, other arithmetic, adam_update(): return (master - learn_rate * update_dir, first_new, second_new)  2.2 us

profile of v1, /device:TPU:0, one launch (start us, length us, event | category | flops | bytes accessed | tf_op | source)
XLA Modules:
  0.0 49.3 jit_solution(4766008668782442370)
XLA Ops:
  0.6 0.0 copy-start
  0.6 0.0 copy-start.1
  0.7 0.0 copy-start.2
  0.7 46.4 %shard_map.121 = f32[160,576]{1,0:T(8,128)} custom-call(bf16[256,1152]{1,0:T(8,128)(2,1)} %tokens_hbm.1, bf16[1152,1152]{1,0:T(8,128)(2,1)} %proj_hbm.1, f32[1152]{0:T(1024)} %mean_hbm.1, bf16[576,1152]{1,0:T(8,128)(2,1)} %bitcast.4, s32[1,256]{1,0:T(1,128)} %bitcast.5, bf16[384,1280]{1,0:T(8,128)(2,1)} %hidden_hbm.1, bf16[576,1280]{1,0:T(8,128)(2,1)} %bitcast.3), custom_call_target="tpu_custom_call" | custom-call | flops 2151677952 | bytes 10485760 | tf_op jit(solution)/shard_map/pallas_call | solution.py:447
  47.0 0.0 copy-done
  47.0 0.0 copy-done.1
  47.1 0.0 copy-done.2
  47.1 2.2 %multiply_subtract_fusion = (f32[160,576]{1,0:T(8,128)}, f32[160,576]{1,0:T(8,128)}, f32[160,576]{1,0:T(8,128)}) fusion(f32[160,576]{1,0:T(8,128)S(1)} %copy-done, f32[160,576]{1,0:T(8,128)} %shard_map.121, f32[160,576]{1,0:T(8,128)S(1)} %copy-done.1, f32[160,576]{1,0:T(8,128)S(1)} %copy-done.2), kind=kLoop, calls=%fused_computation.2 | loop fusion | flops 1290240 | bytes 2580480 | tf_op jit(solution)/shard_map/sub | solution.py:33
Async XLA Ops:
  0.6 46.4 %copy-start = (f32[160,576]{1,0:T(8,128)S(1)}, f32[160,576]{1,0:T(8,128)}, u32[]{:S(2)}) copy-start(f32[160,576]{1,0:T(8,128)} %param.17) | copy-start | bytes 1105924
  0.6 46.4 %copy-start.1 = (f32[160,576]{1,0:T(8,128)S(1)}, f32[160,576]{1,0:T(8,128)}, u32[]{:S(2)}) copy-start(f32[160,576]{1,0:T(8,128)} %param.19) | copy-start | bytes 1105924
  0.7 46.4 %copy-start.2 = (f32[160,576]{1,0:T(8,128)S(1)}, f32[160,576]{1,0:T(8,128)}, u32[]{:S(2)}) copy-start(f32[160,576]{1,0:T(8,128)} %param.18) | copy-start | bytes 1105924

commit v2 on v1

--- a/solution.py
+++ b/solution.py
@@ -157,7 +157,6 @@
     cap = slots // SPANS
     block = width // SHARDS
     group = width // 2
-    half = block // 2
 
     pairs = (
         (tokens_hbm, tokens),
@@ -257,11 +256,11 @@
         return copy
 
     class Pair:
-        def __init__(self, c, src, dst, sems, device):
+        def __init__(self, sources, targets, sems, device):
             self.copies = [
                 pltpu.make_async_remote_copy(
-                    src_ref=buf[c][src + 6 * i],
-                    dst_ref=buf[c][dst + 6 * i],
+                    src_ref=sources[i],
+                    dst_ref=targets[i],
                     send_sem=sems[i],
                     recv_sem=sems[2 + i],
                     device_id=device,
@@ -281,12 +280,6 @@
         def wait_send(self):
             for copy in self.copies:
                 copy.wait_send()
-
-    def put(values, c, at):
-        encode(values, buf[c][at], buf[c][at + 6])
-
-    def get(c, at):
-        return decode(buf[c][at], buf[c][at + 6])
 
     core_copies = {}
     plane_copies = {}
@@ -324,48 +317,63 @@
                 (span, mate),
             )
 
-    def z_send(c, stage):
-        at = 7 + 2 * stage
+    n = len(chunks)
+    z_low = (lax.rem(span, 2) == 0, span < 2)
+
+    def parts(c, at):
+        return buf[c][7].at[at], buf[c][8].at[at]
+
+    def z_send(c, stage, source, target, device):
         z_copies[c, stage] = Pair(
-            c, at, at + 1, [z_sem.at[c, stage, i] for i in range(4)], (z_mates[stage % 2], me)
+            parts(c, source),
+            parts(c, target),
+            [z_sem.at[c, stage, i] for i in range(4)],
+            (device, me),
         )
         z_copies[c, stage].start()
 
-    odd = lax.rem(span, 2)
-    kept_half = pl.ds(pl.multiple_of(odd * half, 16), half)
-    given_half = pl.ds(pl.multiple_of((1 - odd) * half, 16), half)
+    def at_once(c):
+        return c >= n - 2
+
+    def z_sum(c, stage):
+        z_copies[c, stage].wait_recv()
+        mine, other = decode(*parts(c, 2 * stage)), decode(*parts(c, 2 * stage + 1))
+        low = jnp.where(z_low[stage], mine, other)
+        high = jnp.where(z_low[stage], other, mine)
+        return low + high
 
     def first_z(c):
-        core_in, total, plane_in, own = buf[c][3], buf[c][4], buf[c][6], buf[c][19]
+        core_in, total, plane_in = buf[c][3], buf[c][4], buf[c][6]
         here = rows_of(me // 2)
         value = total[here, :] + core_in[here, :]
         for j in range(3):
             plane_copies[c, j].wait_recv()
             value = value + plane_in[j]
-        own[...] = value
-        put(own[given_half, :], c, 7)
-        z_send(c, 0)
+        if at_once(c):
+            encode(value, *parts(c, span))
+            for j, step in enumerate((2, 3, 1)):
+                z_send(c, j, span, span, lax.rem(span + step, SPANS))
+        else:
+            encode(value, *parts(c, 0))
+            z_send(c, 0, 0, 1, z_mates[0])
 
     def second_z(c):
-        z_copies[c, 0].wait_recv()
-        put(buf[c][19][kept_half, :] + get(c, 8), c, 9)
-        z_send(c, 1)
-
-    def third_z(c):
-        z_copies[c, 1].wait_recv()
-        mine, other = get(c, 9), get(c, 10)
-        low = jnp.where(span < 2, mine, other)
-        high = jnp.where(span < 2, other, mine)
-        put(low + high, c, 11)
-        z_send(c, 2)
+        if not at_once(c):
+            encode(z_sum(c, 0), *parts(c, 2))
+            z_send(c, 1, 2, 3, z_mates[1])
 
     def finish(c):
         lo, hi = chunks[c]
-        z_copies[c, 2].wait_recv()
-        out[kept_half, lo:hi] = get(c, 11)
-        out[given_half, lo:hi] = get(c, 12)
-
-    n = len(chunks)
+        if at_once(c):
+            for j in range(3):
+                z_copies[c, j].wait_recv()
+            sum_z = decode(*parts(c, 0))
+            for j in range(1, SPANS):
+                sum_z = sum_z + decode(*parts(c, j))
+        else:
+            sum_z = z_sum(c, 1)
+        out[:, lo:hi] = sum_z
+
     for c in range(n):
         form(c)
         if c >= 1:
@@ -374,13 +382,10 @@
             second_z(c - 2)
         plane(c)
         if c >= 3:
-            third_z(c - 3)
-        if c >= 4:
-            finish(c - 4)
-    for c in range(n, n + 4):
-        for stage, step in ((2, second_z), (1, first_z), (3, third_z), (4, finish)):
-            if 0 <= c - stage < n:
-                step(c - stage)
+            finish(c - 3)
+    first_z(n - 1)
+    for c in range(n - 3, n):
+        finish(c)
 
     for copy in a2a:
         copy.wait_send()
@@ -429,9 +434,8 @@
         scratch += [pltpu.VMEM((width // 2, wide), bf16)] * 2
         scratch += [pltpu.VMEM((width // 2, wide), f32)]
         scratch += [pltpu.VMEM((3, block, wide), bf16)] * 2
-        scratch += [pltpu.VMEM((block // 2, wide), jnp.int16)] * 6
-        scratch += [pltpu.VMEM((8, 128), f32)] * 6
-        scratch += [pltpu.VMEM((block, wide), f32)]
+        scratch += [pltpu.VMEM((SPANS, block, wide), jnp.int16)]
+        scratch += [pltpu.VMEM((SPANS, 8, 128), f32)]
     n = len(chunks)
     dma = pltpu.SemaphoreType.DMA
     scratch += [

time: 49.4 us -> 45.2 us (0.915)
  Pallas kernels: 46.4 us -> 42.2 us
    pallas_call x1, Pallas kernels: 46.4 us -> 42.2 us  [kernel_body(): pl.pallas_call(functools.partial(step_kernel, chunks), out_shape=jax.Shap...]
where the time goes in v2:
time: 45.2 us; the launch traced here: 45.1 us
  Pallas kernels  42.2 us (93%)
  other arithmetic  2.2 us (5%)
  between operations  0.69 us (2%)
    pallas_call x1, Pallas kernels, kernel_body(): pl.pallas_call(functools.partial(step_kernel, chunks), out_shape=jax.Shap...  42.2 us
    sub x1, other arithmetic, adam_update(): return (master - learn_rate * update_dir, first_new, second_new)  2.2 us

profile of v2, /device:TPU:0, one launch (start us, length us, event | category | flops | bytes accessed | tf_op | source)
XLA Modules:
  0.0 45.1 jit_solution(6005014749942017957)
XLA Ops:
  0.6 0.0 copy-start
  0.6 0.0 copy-start.1
  0.7 0.0 copy-start.2
  0.7 42.2 %shard_map.121 = f32[160,576]{1,0:T(8,128)} custom-call(bf16[256,1152]{1,0:T(8,128)(2,1)} %tokens_hbm.1, bf16[1152,1152]{1,0:T(8,128)(2,1)} %proj_hbm.1, f32[1152]{0:T(1024)} %mean_hbm.1, bf16[576,1152]{1,0:T(8,128)(2,1)} %bitcast.4, s32[1,256]{1,0:T(1,128)} %bitcast.5, bf16[384,1280]{1,0:T(8,128)(2,1)} %hidden_hbm.1, bf16[576,1280]{1,0:T(8,128)(2,1)} %bitcast.3), custom_call_target="tpu_custom_call" | custom-call | flops 2151677952 | bytes 10485760 | tf_op jit(solution)/shard_map/pallas_call | solution.py:451
  42.9 0.0 copy-done
  42.9 0.0 copy-done.1
  42.9 0.0 copy-done.2
  42.9 2.2 %multiply_subtract_fusion = (f32[160,576]{1,0:T(8,128)}, f32[160,576]{1,0:T(8,128)}, f32[160,576]{1,0:T(8,128)}) fusion(f32[160,576]{1,0:T(8,128)S(1)} %copy-done, f32[160,576]{1,0:T(8,128)} %shard_map.121, f32[160,576]{1,0:T(8,128)S(1)} %copy-done.1, f32[160,576]{1,0:T(8,128)S(1)} %copy-done.2), kind=kLoop, calls=%fused_computation.2 | loop fusion | flops 1290240 | bytes 2580480 | tf_op jit(solution)/shard_map/sub | solution.py:33
Async XLA Ops:
  0.6 42.2 %copy-start = (f32[160,576]{1,0:T(8,128)S(1)}, f32[160,576]{1,0:T(8,128)}, u32[]{:S(2)}) copy-start(f32[160,576]{1,0:T(8,128)} %param.17) | copy-start | bytes 1105924
  0.6 42.2 %copy-start.1 = (f32[160,576]{1,0:T(8,128)S(1)}, f32[160,576]{1,0:T(8,128)}, u32[]{:S(2)}) copy-start(f32[160,576]{1,0:T(8,128)} %param.19) | copy-start | bytes 1105924
  0.7 42.2 %copy-start.2 = (f32[160,576]{1,0:T(8,128)S(1)}, f32[160,576]{1,0:T(8,128)}, u32[]{:S(2)}) copy-start(f32[160,576]{1,0:T(8,128)} %param.18) | copy-start | bytes 1105924

commit v3 on v2

--- a/solution.py
+++ b/solution.py
@@ -88,7 +88,7 @@
 
 
 def chunks_of(features):
-    return tuple((lo, min(lo + 128, features)) for lo in range(0, features, 128))
+    return ((0, 256),) + tuple((lo, min(lo + 128, features)) for lo in range(256, features, 128))
 
 
 def dot(a, b):

time: 45.2 us -> 46.1 us (1.020)
  Pallas kernels: 42.2 us -> 43.1 us
    pallas_call x1, Pallas kernels: 42.2 us -> 43.1 us  [kernel_body(): pl.pallas_call(functools.partial(step_kernel, chunks), out_shape=jax.Shap...]
where the time goes in v3:
time: 46.1 us; the launch traced here: 46 us
  Pallas kernels  43.1 us (93%)
  other arithmetic  2.2 us (5%)
  between operations  0.69 us (1%)
    pallas_call x1, Pallas kernels, kernel_body(): pl.pallas_call(functools.partial(step_kernel, chunks), out_shape=jax.Shap...  43.1 us
    sub x1, other arithmetic, adam_update(): return (master - learn_rate * update_dir, first_new, second_new)  2.2 us

profile of v3, /device:TPU:0, one launch (start us, length us, event | category | flops | bytes accessed | tf_op | source)
XLA Modules:
  0.0 46.0 jit_solution(13150641630836599876)
XLA Ops:
  0.6 0.0 copy-start
  0.6 0.0 copy-start.1
  0.7 0.0 copy-start.2
  0.7 43.1 %shard_map.121 = f32[160,576]{1,0:T(8,128)} custom-call(bf16[256,1152]{1,0:T(8,128)(2,1)} %tokens_hbm.1, bf16[1152,1152]{1,0:T(8,128)(2,1)} %proj_hbm.1, f32[1152]{0:T(1024)} %mean_hbm.1, bf16[576,1152]{1,0:T(8,128)(2,1)} %bitcast.4, s32[1,256]{1,0:T(1,128)} %bitcast.5, bf16[384,1280]{1,0:T(8,128)(2,1)} %hidden_hbm.1, bf16[576,1280]{1,0:T(8,128)(2,1)} %bitcast.3), custom_call_target="tpu_custom_call" | custom-call | flops 2151677952 | bytes 10485760 | tf_op jit(solution)/shard_map/pallas_call | solution.py:451
  43.8 0.0 copy-done
  43.8 0.0 copy-done.1
  43.8 0.0 copy-done.2
  43.8 2.2 %multiply_subtract_fusion = (f32[160,576]{1,0:T(8,128)}, f32[160,576]{1,0:T(8,128)}, f32[160,576]{1,0:T(8,128)}) fusion(f32[160,576]{1,0:T(8,128)S(1)} %copy-done, f32[160,576]{1,0:T(8,128)} %shard_map.121, f32[160,576]{1,0:T(8,128)S(1)} %copy-done.1, f32[160,576]{1,0:T(8,128)S(1)} %copy-done.2), kind=kLoop, calls=%fused_computation.2 | loop fusion | flops 1290240 | bytes 2580480 | tf_op jit(solution)/shard_map/sub | solution.py:33
Async XLA Ops:
  0.6 43.1 %copy-start = (f32[160,576]{1,0:T(8,128)S(1)}, f32[160,576]{1,0:T(8,128)}, u32[]{:S(2)}) copy-start(f32[160,576]{1,0:T(8,128)} %param.17) | copy-start | bytes 1105924
  0.6 43.1 %copy-start.1 = (f32[160,576]{1,0:T(8,128)S(1)}, f32[160,576]{1,0:T(8,128)}, u32[]{:S(2)}) copy-start(f32[160,576]{1,0:T(8,128)} %param.19) | copy-start | bytes 1105924
  0.7 43.1 %copy-start.2 = (f32[160,576]{1,0:T(8,128)S(1)}, f32[160,576]{1,0:T(8,128)}, u32[]{:S(2)}) copy-start(f32[160,576]{1,0:T(8,128)} %param.18) | copy-start | bytes 1105924
